TPU v7x, 32 devices: a whole 2x2x4 slice. The times are simulated.
32 devices in a mesh: row: 4 (over y, x), col: 8 (over z, core).
Axes of the slice: x: 2, y: 2, z: 4, core: 2. Of those that a mesh axis runs over, the one named last changes fastest.
Arguments:
- rhs: float32 [4, 4, 8, 128, 256], P(None, 'row', 'col'), may hold values from -6 to 6
- diag_inverse: float32 [4, 4, 8, 128, 128], P(None, 'row', 'col'), as said below
- update_blocks: float32 [3, 4, 8, 48, 128, 128], P(None, 'row', 'col'), may hold values from -0.15625 to 0.15625
- source_slot: int32 [3, 4, 8, 48], P(None, 'row', 'col'), may hold values from 0 to 3
- target_slot: int32 [3, 4, 8, 48], P(None, 'row', 'col'), may hold values from 0 to 7
- block_count: int32 [3, 4, 8], P(None, 'row', 'col'), may hold values from 1 to 48, as said below
Outputs:
- forward_solution: float32 [4, 4, 8, 128, 256], P(None, 'row', 'col')
- solution: float32 [4, 4, 8, 128, 256], P(None, 'row', 'col')
Inputs may be any that keep to these rules, and one draw needn't show every extreme that they name: Each diag_inverse block is lower triangular with diagonal entries between 0.5 and 1.6. `block_count`: at every level some device uses all 48 slots.
All inputs are finite; a program needn't handle non-finite values.
Results may differ from a plain program's by a relative error of at most 0.0003.
Values sent between devices are 32-bit elements; how exact they have to be, the bound alone decides.
A program may use at most 128 MiB of HBM per device.

v0:
```python
import math

import jax
import jax.numpy as jnp
from jax import lax
from jax.sharding import PartitionSpec as P


def apply_inverse(inverse, values):
    return jnp.einsum("...st,...tn->...sn", inverse, values, precision=lax.Precision.HIGHEST)


def apply_transposed(inverse, values):
    return jnp.einsum("...ts,...tn->...sn", inverse, values, precision=lax.Precision.HIGHEST)


def block_terms(tile_stack, picked, placed, filled, operand, totals, transposed):
    slot_count = tile_stack.shape[0]
    group_size = math.gcd(slot_count, 8)
    rounds = (filled + group_size - 1) // group_size

    def advance(number, running):
        offset = number * group_size
        tile_group = lax.dynamic_slice_in_dim(tile_stack, offset, group_size, 0)
        chosen_rows = lax.dynamic_slice_in_dim(picked, offset, group_size, 0)
        target_rows = lax.dynamic_slice_in_dim(placed, offset, group_size, 0)
        active = (offset + jnp.arange(group_size, dtype=jnp.int32) < filled).astype(jnp.float32)
        selected = operand[chosen_rows]
        if transposed:
            products = jnp.einsum(
                "gts,gtn->gsn", tile_group, selected, precision=lax.Precision.HIGHEST
            )
        else:
            products = jnp.einsum(
                "gst,gtn->gsn", tile_group, selected, precision=lax.Precision.HIGHEST
            )
        return running.at[target_rows].add(products * active[:, None, None])

    return lax.fori_loop(0, rounds, advance, totals)


def per_device(rhs, diag_inverse, update_blocks, source_slot, target_slot, block_count):
    levels = rhs.shape[0]
    last_level = levels - 1
    rhs_local = rhs[:, 0, 0]
    inverse_local = diag_inverse[:, 0, 0]
    tiles_local = update_blocks[:, 0, 0]
    sources_local = source_slot[:, 0, 0]
    targets_local = target_slot[:, 0, 0]
    filled_local = block_count[:, 0, 0]
    row_count = lax.axis_size("row")
    col_count = lax.axis_size("col")
    block_shape = rhs_local.shape[1:]
    forward = [apply_inverse(inverse_local[0], rhs_local[0])]
    for level_index in range(1, levels):
        forward_gathered = lax.all_gather(forward[-1][None], "row", axis=0, tiled=True)
        forward_zero_terms = jnp.zeros((col_count,) + block_shape, jnp.float32)
        owner_reduced = lax.psum_scatter(
            block_terms(
                tiles_local[level_index - 1],
                sources_local[level_index - 1],
                targets_local[level_index - 1],
                filled_local[level_index - 1],
                forward_gathered,
                forward_zero_terms,
                False,
            ),
            "col",
            scatter_dimension=0,
            tiled=True,
        )
        forward.append(
            apply_inverse(inverse_local[level_index], rhs_local[level_index] - owner_reduced[0])
        )
    backward = [apply_transposed(inverse_local[last_level], forward[-1])]
    for level_index in range(last_level - 1, -1, -1):
        gathered = lax.all_gather(backward[0][None], "col", axis=0, tiled=True)
        solved = forward[level_index]
        zero_terms = jnp.zeros((row_count,) + block_shape, jnp.float32)
        totals = block_terms(
            tiles_local[level_index],
            targets_local[level_index],
            sources_local[level_index],
            filled_local[level_index],
            gathered,
            zero_terms,
            True,
        )
        reduced = lax.psum_scatter(totals, "row", scatter_dimension=0, tiled=True)
        backward.insert(0, apply_transposed(inverse_local[level_index], solved - reduced[0]))
    forward_out = jnp.stack(forward)[:, None, None]
    backward_out = jnp.stack(backward)[:, None, None]
    return (forward_out, backward_out)


def solution(mesh):
    in_specs = (
        P(None, "row", "col", None, None),
        P(None, "row", "col", None, None),
        P(None, "row", "col", None, None, None),
        P(None, "row", "col", None),
        P(None, "row", "col", None),
        P(None, "row", "col"),
    )
    out_specs = (P(None, "row", "col", None, None), P(None, "row", "col", None, None))
    return jax.shard_map(
        per_device, mesh=mesh, in_specs=in_specs, out_specs=out_specs, check_vma=False
    )
```

profile of v0, /device:TPU:0, one launch (start us, length us, event | category | flops | bytes accessed | tf_op | source)
XLA Modules:
  0.0 540.7 jit_solution(7285897336197406575)
XLA Ops:
  7.2 1.4 fusion.46
  9.3 7.6 %fusion.45 = (f32[1,1,1,48,128,128]{5,4,3,2,1,0:T(8,128)S(1)}, f32[1,1,1,48,128,128]{5,4,3,2,1,0:T(8,128)}, f32[1,1,1,48,128,128]{5,4,3,2,1,0:T(8,128)}) fusion(f32[3,1,1,48,128,128]{5,4,3,2,1,0:T(8,128)} %param.20), kind=kLoop, calls=%fused_computation.102 | loop fusion | bytes 18874368 | tf_op jit(solution)/shard_map/slice | solution.py:60
  16.9 2.3 copy.44
  20.4 11.5 %all-gather = f32[512,256]{1,0:T(8,128)S(1)} all-gather(f32[128,256]{1,0:T(8,128)S(1)} %fusion.20), channel_id=2, replica_groups=mesh['row'=4,'col'=8] {'row'}, dimensions={0}, use_global_device_ids=true | all-gather | bytes 655360 | tf_op jit(solution)/shard_map/all_gather | solution.py:56
  33.1 6.8 %while.60 = (s32[]{:T(128)}, f32[8,128,256]{2,1,0:T(8,128)}, s32[]{:T(128)}, s32[48]{0:T(128)S(1)}, f32[48,128,128]{1,2,0:T(8,128)}, /*index=5*/s32[48]{0:T(128)...) while((s32[]{:T(128)}, f32[8,128,256]{2,1,0:T(8,128)}, ...), condition=%wide.region_2.3_spmd, body=%wide.region_0.2_spmd.sunk | while | flops 403178560 | bytes 7868883 | solution.py:39
  34.4 2.1 convolution_multiply_fusion.12
  36.6 3.3 scatter_fusion
  40.6 3.6 copy.45
  44.2 58.6 %reduce-scatter.13.cloned.1.call-done = f32[1,128,256]{2,1,0:T(8,128)} async-done(((f32[8,128,256]{2,1,0:T(8,128)}), f32[1,128,256]{2,1,0:T(8,128)}) %reduce-scatter.13.cloned.1.call-update) | async-done | bytes 131088 | tf_op jit(solution)/shard_map/reduce_scatter | solution.py:58
  104.1 10.4 %all-gather.1 = f32[512,256]{1,0:T(8,128)S(1)} all-gather(f32[128,256]{1,0:T(8,128)S(1)} %bitcast.147), channel_id=3, replica_groups=mesh['row'=4,'col'=8] {'row'}, dimensions={0}, use_global_device_ids=true | all-gather | bytes 655360 | tf_op jit(solution)/shard_map/all_gather | solution.py:56
  115.6 41.0 %while.61 = (s32[]{:T(128)}, f32[8,128,256]{2,1,0:T(8,128)}, s32[]{:T(128)}, s32[48]{0:T(128)S(1)}, f32[48,128,128]{1,2,0:T(8,128)}, /*index=5*/s32[48]{0:T(128)...) while((s32[]{:T(128)}, f32[8,128,256]{2,1,0:T(8,128)}, ...), condition=%wide.region_6.7_spmd, body=%wide.region_4.6_spmd.sunk | while | flops 403178560 | bytes 7868883 | solution.py:39
  117.0 2.1 convolution_multiply_fusion.13
  119.1 3.3 scatter_fusion.1
  123.9 2.1 convolution_multiply_fusion.13
  126.0 3.3 scatter_fusion.1
  130.7 2.1 convolution_multiply_fusion.13
  132.9 3.3 scatter_fusion.1
  137.6 2.1 convolution_multiply_fusion.13
  139.7 3.3 scatter_fusion.1
  144.4 2.1 convolution_multiply_fusion.13
  146.6 3.3 scatter_fusion.1
  151.3 2.1 convolution_multiply_fusion.13
  153.4 3.2 scatter_fusion.1
  157.2 3.5 copy.46
  160.8 25.3 %reduce-scatter.15.cloned.1.call-done = f32[1,128,256]{2,1,0:T(8,128)} async-done(((f32[8,128,256]{2,1,0:T(8,128)}), f32[1,128,256]{2,1,0:T(8,128)}) %reduce-scatter.15.cloned.1.call-update) | async-done | bytes 131088 | tf_op jit(solution)/shard_map/reduce_scatter | solution.py:58
  187.3 10.2 %all-gather.2 = f32[512,256]{1,0:T(8,128)S(1)} all-gather(f32[128,256]{1,0:T(8,128)S(1)} %bitcast.149), channel_id=4, replica_groups=mesh['row'=4,'col'=8] {'row'}, dimensions={0}, use_global_device_ids=true | all-gather | bytes 655360 | tf_op jit(solution)/shard_map/all_gather | solution.py:56
  198.6 13.4 %while.62 = (s32[]{:T(128)}, f32[8,128,256]{2,1,0:T(8,128)}, s32[]{:T(128)}, s32[48]{0:T(128)S(1)}, f32[48,128,128]{1,2,0:T(8,128)}, /*index=5*/s32[48]{0:T(128)...) while((s32[]{:T(128)}, f32[8,128,256]{2,1,0:T(8,128)}, ...), condition=%wide.region_10.11_spmd, body=%wide.region_8.10_spmd.sunk | while | flops 403178560 | bytes 7868883 | solution.py:39
  199.8 2.1 convolution_multiply_fusion.14
  202.0 3.3 scatter_fusion.2
  206.5 2.1 convolution_multiply_fusion.14
  208.7 3.3 scatter_fusion.2
  212.0 56.0 %reduce-scatter.17.cloned.1.call-done = f32[1,128,256]{2,1,0:T(8,128)} async-done(((f32[8,128,256]{2,1,0:T(8,128)}), f32[1,128,256]{2,1,0:T(8,128)}) %reduce-scatter.17.cloned.1.call-update) | async-done | bytes 131088 | tf_op jit(solution)/shard_map/reduce_scatter | solution.py:58
  270.4 22.4 %all-gather.10.cloned.1.call-done = f32[1024,256]{0,1:T(8,128)} async-done(((f32[128,256]{0,1:T(8,128)}), f32[1024,256]{0,1:T(8,128)}) %all-gather.10.cloned.1.call-update) | async-done | bytes 1048592 | tf_op jit(solution)/shard_map/all_gather | solution.py:77
  292.7 2.6 copy.38
  295.4 12.0 %while.63 = (s32[]{:T(128)}, f32[4,128,256]{2,1,0:T(8,128)S(1)}, s32[]{:T(128)}, s32[48]{0:T(128)S(1)}, f32[48,128,128]{1,2,0:T(8,128)}, /*index=5*/s32[48]{0:T(...) while((s32[]{:T(128)}, f32[4,128,256]{2,1,0:T(8,128)S(1)}, ...), condition=%wide.region_14.15_spmd, body=%wide.region_12.14_spmd.sunk | while | flops 403178560 | bytes 7868883 | solution.py:39
  295.6 1.8 gather_fusion.3
  298.1 2.1 convolution_multiply_fusion.15
  301.6 1.8 gather_fusion.3
  304.0 2.1 convolution_multiply_fusion.15
  308.3 45.0 %reduce-scatter.19.cloned.1.call-done = f32[1,128,256]{2,1,0:T(8,128)} async-done(((f32[4,128,256]{2,1,0:T(8,128)}), f32[1,128,256]{2,1,0:T(8,128)}) %reduce-scatter.19.cloned.1.call-update) | async-done | bytes 131088
  353.3 1.9 fusion.13
  355.3 24.1 %all-gather.12.cloned.1.call-done = f32[1024,256]{0,1:T(8,128)} async-done(((f32[128,256]{0,1:T(8,128)}), f32[1024,256]{0,1:T(8,128)}) %all-gather.12.cloned.1.call-update) | async-done | bytes 1048592 | tf_op jit(solution)/shard_map/all_gather | solution.py:77
  379.3 2.6 copy.39
  381.9 36.3 %while.64 = (s32[]{:T(128)}, f32[4,128,256]{2,1,0:T(8,128)S(1)}, s32[]{:T(128)}, s32[48]{0:T(128)S(1)}, f32[48,128,128]{1,2,0:T(8,128)}, /*index=5*/s32[48]{0:T(...) while((s32[]{:T(128)}, f32[4,128,256]{2,1,0:T(8,128)S(1)}, ...), condition=%wide.region_18.19_spmd, body=%wide.region_16.18_spmd.sunk | while | flops 403178560 | bytes 7868883 | solution.py:39
  382.1 1.8 gather_fusion.4
  384.6 2.1 convolution_multiply_fusion.16
  388.1 1.8 gather_fusion.4
  390.7 2.1 convolution_multiply_fusion.16
  394.2 1.8 gather_fusion.4
  396.7 2.1 convolution_multiply_fusion.16
  400.2 1.8 gather_fusion.4
  402.8 2.1 convolution_multiply_fusion.16
  406.3 1.8 gather_fusion.4
  408.8 2.1 convolution_multiply_fusion.16
  412.3 1.8 gather_fusion.4
  414.9 2.1 convolution_multiply_fusion.16
  419.2 23.5 %reduce-scatter.21.cloned.1.call-done = f32[1,128,256]{2,1,0:T(8,128)} async-done(((f32[4,128,256]{2,1,0:T(8,128)}), f32[1,128,256]{2,1,0:T(8,128)}) %reduce-scatter.21.cloned.1.call-update) | async-done | bytes 131088
  442.7 2.0 fusion.12
  444.7 24.1 %all-gather.14.cloned.1.call-done = f32[1024,256]{0,1:T(8,128)} async-done(((f32[128,256]{0,1:T(8,128)}), f32[1024,256]{0,1:T(8,128)}) %all-gather.14.cloned.1.call-update) | async-done | bytes 1048592 | tf_op jit(solution)/shard_map/all_gather | solution.py:77
  468.8 2.6 copy.40
  471.4 6.1 %while.65 = (s32[]{:T(128)}, f32[4,128,256]{2,1,0:T(8,128)S(1)}, s32[]{:T(128)}, s32[48]{0:T(128)S(1)}, f32[48,128,128]{1,2,0:T(8,128)}, /*index=5*/s32[48]{0:T(...) while((s32[]{:T(128)}, f32[4,128,256]{2,1,0:T(8,128)S(1)}, ...), condition=%wide.region_22.23_spmd, body=%wide.region_20.22_spmd.sunk | while | flops 403178560 | bytes 7868883 | solution.py:39
  471.5 1.9 gather_fusion.5
  474.1 2.1 convolution_multiply_fusion.17
  479.2 52.6 %reduce-scatter.23.cloned.1.call-done = f32[1,128,256]{2,1,0:T(8,128)} async-done(((f32[4,128,256]{2,1,0:T(8,128)}), f32[1,128,256]{2,1,0:T(8,128)}) %reduce-scatter.23.cloned.1.call-update) | async-done | bytes 131088
  (125 shorter events, 46.4 us)
Async XLA Ops:
  7.2 95.7 %reduce-scatter.13.cloned.1.call-start = ((), (), s32[]{:S(2)}) async-start(), calls=%async_computation.6 | async-start | bytes 1179648 | tf_op jit(solution)/shard_map/reduce_scatter | solution.py:58
  16.9 2.3 copy-start.6
  16.9 15.0 %copy-start.7 = (s32[3,1,1,48]{3,2,1,0:T(1,128)S(1)}, s32[3,1,1,48]{3,2,1,0:T(1,128)}, u32[]{:S(2)}) copy-start(s32[3,1,1,48]{3,2,1,0:T(1,128)} %param.21) | copy-start | bytes 1732
  16.9 15.0 %copy-start.8 = (s32[3,1,1,48]{3,2,1,0:T(1,128)S(1)}, s32[3,1,1,48]{3,2,1,0:T(1,128)}, u32[]{:S(2)}) copy-start(s32[3,1,1,48]{3,2,1,0:T(1,128)} %param.22) | copy-start | bytes 1732
  39.9 146.2 %reduce-scatter.15.cloned.1.call-start = ((), (), s32[]{:S(2)}) async-start(), calls=%async_computation.7 | async-start | bytes 1179648 | tf_op jit(solution)/shard_map/reduce_scatter | solution.py:58
  156.6 111.4 %reduce-scatter.17.cloned.1.call-start = ((), (), s32[]{:S(2)}) async-start(), calls=%async_computation.8 | async-start | bytes 1179648 | tf_op jit(solution)/shard_map/reduce_scatter | solution.py:58
  212.0 80.8 %all-gather.10.cloned.1.call-start = ((), (), s32[]{:S(2)}) async-start(), calls=%async_computation.9 | async-start | bytes 1179648 | tf_op jit(solution)/shard_map/all_gather | solution.py:77
  270.3 82.9 %reduce-scatter.19.cloned.1.call-start = ((), (), s32[]{:S(2)}) async-start(), calls=%async_computation.12 | async-start | bytes 655360
  307.4 0.8 copy-start.1
  308.2 71.1 %all-gather.12.cloned.1.call-start = ((), (), s32[]{:S(2)}) async-start(), calls=%async_computation.10 | async-start | bytes 1179648 | tf_op jit(solution)/shard_map/all_gather | solution.py:77
  355.2 87.5 %reduce-scatter.21.cloned.1.call-start = ((), (), s32[]{:S(2)}) async-start(), calls=%async_computation.13 | async-start | bytes 655360
  418.3 0.8 copy-start.2
  419.1 49.6 %all-gather.14.cloned.1.call-start = ((), (), s32[]{:S(2)}) async-start(), calls=%async_computation.11 | async-start | bytes 1179648 | tf_op jit(solution)/shard_map/all_gather | solution.py:77
  444.7 87.1 %reduce-scatter.23.cloned.1.call-start = ((), (), s32[]{:S(2)}) async-start(), calls=%async_computation.14 | async-start | bytes 655360
  471.4 61.7 %copy-start.3 = (f32[256,128]{1,0:T(8,128)S(1)}, f32[256,128]{1,0:T(8,128)}, u32[]{:S(2)}) copy-start(f32[256,128]{1,0:T(8,128)} %fusion.13) | copy-start | bytes 393220
  471.4 61.7 %copy-start.4 = (f32[256,128]{1,0:T(8,128)S(1)}, f32[256,128]{1,0:T(8,128)}, u32[]{:S(2)}) copy-start(f32[256,128]{1,0:T(8,128)} %fusion.12) | copy-start | bytes 393220
  471.4 61.7 %copy-start.5 = (f32[256,128]{1,0:T(8,128)S(1)}, f32[256,128]{1,0:T(8,128)}, u32[]{:S(2)}) copy-start(f32[256,128]{1,0:T(8,128)} %fusion.26) | copy-start | bytes 393220
  477.5 0.8 copy-start
Sparse Core Ops, SparseCore 0:
  40.0 62.7 reduce-scatter.12
  156.7 29.2 reduce-scatter.14
  212.1 55.8 reduce-scatter.16
  270.4 22.2 all-gather.9
  308.3 44.8 reduce-scatter.18
  355.3 23.9 all-gather.11
  419.2 23.3 reduce-scatter.20
  444.8 23.9 all-gather.13
  478.4 53.3 reduce-scatter.22
where the time goes:
time: 545 us; the launch traced here: 541 us
  waiting for transfers between devices  332 us (61%)
  other arithmetic  55.7 us (10%)
  local copies, waits for them, and re-layouts  55.2 us (10%)
  matrix products  48.8 us (9%)
  blocking collectives  32 us (6%)
  between operations  16 us (3%)
    reduce_scatter x3, waiting for transfers between devices, per_device(): lax.psum_scatter(block_terms(tiles_local[level_index - 1], sources_local[...  140 us
    unnamed x12, waiting for transfers between devices  121 us
    all_gather x3, waiting for transfers between devices, per_device(): gathered = lax.all_gather(backward[0][None], 'col', axis=0, tiled=True)  70.5 us
    scatter-add x18, other arithmetic, advance(): return running.at[target_rows].add(products * active[:, None, None])  41.4 us
    all_gather x3, blocking collectives, per_device(): lax.all_gather(forward[-1][None], 'row', axis=0, tiled=True)  32 us
    gather x18, local copies, waits for them, and re-layouts, advance(): selected = operand[chosen_rows]  22.1 us
    dot_general x9, matrix products, advance(): jnp.einsum('gst,gtn->gsn', tile_group, selected, precision=lax.Precision....  19.2 us
    dot_general x9, matrix products, advance(): jnp.einsum('gts,gtn->gsn', tile_group, selected, precision=lax.Precision....  18.6 us
  transfers between devices with their start and end apart: 9, of which 9 were waited for; matrix products, arithmetic and copies ran while one was open for 1% of the time, Pallas kernels for 0%

commit v1 on v0

v1 whole, which is shorter than its diff:
```python
import functools

import jax
import jax.numpy as jnp
from jax import lax
from jax.experimental import pallas as pl
from jax.experimental.pallas import tpu as pltpu
from jax.sharding import PartitionSpec as P

F32, BF16 = jnp.float32, jnp.bfloat16
MESH = pl.DeviceIdType.MESH
VMEM_BYTES = 60 * 1024 * 1024


def split(x):
    high = x.astype(BF16)
    return high, (x - high.astype(F32)).astype(BF16)


def dot(a, b):
    return jnp.dot(a, b, preferred_element_type=F32)


def merge_kernel(rows, cols, src, tgt, count, blocks, out, acc):
    level, part = pl.program_id(0), pl.program_id(1)
    width = blocks.shape[-1]
    acc[...] = jnp.zeros_like(acc)

    def add(b, _):
        t = tgt[level, b] - part * cols
        s = src[level, b]

        @pl.when((t >= 0) & (t < cols))
        def _():
            i = t * rows + s
            acc[i] += blocks[0, b]

        return 0

    lax.fori_loop(0, count[level], add, 0)

    def write(t, _):
        for s in range(rows):
            high, low = split(acc[t * rows + s])
            out[0, t, 0, :, s * width : (s + 1) * width] = high
            out[0, t, 1, :, s * width : (s + 1) * width] = low
        return 0

    lax.fori_loop(0, cols, write, 0)


def merge(blocks, src, tgt, count, rows, cols):
    steps, slots, width, _ = blocks.shape
    parts = max(1, rows * cols // 64)
    per = cols // parts
    return pl.pallas_call(
        functools.partial(merge_kernel, rows, per),
        grid=(steps, parts),
        out_shape=jax.ShapeDtypeStruct((steps, cols, 2, width, rows * width), BF16),
        in_specs=[pl.BlockSpec(memory_space=pltpu.SMEM)] * 3
        + [pl.BlockSpec((1, slots, width, width), lambda l, p: (l, 0, 0, 0))],
        out_specs=pl.BlockSpec((1, per, 2, width, rows * width), lambda l, p: (l, p, 0, 0, 0)),
        scratch_shapes=[pltpu.VMEM((per * rows, width, width), F32)],
        compiler_params=pltpu.CompilerParams(vmem_limit_bytes=VMEM_BYTES),
    )(src, tgt, count, blocks)


def solve_kernel(
    rows, cols, halves, rhs, dinv, g_hbm, f_out, s_out,
    g, fg, psib, rsib, pown, rz, zg, q, rq, yt,
    g_sem, row_s, row_r, sib_s, sib_r, z_s, z_r,
    bz_s, bz_r, bsib_s, bsib_r, brow_s, brow_r,
):
    levels, _, _, S, total = rhs.shape
    n = total // halves
    steps = levels - 1
    chips = cols // 2
    kept = g.shape[0]
    me_r, me_c = lax.axis_index("row"), lax.axis_index("col")
    z, k = me_c // 2, me_c % 2
    sib = (me_r, 2 * z + 1 - k)
    unroll = rows * cols <= 32

    def row_dev(d):
        return (lax.rem(me_r + d, rows), me_c)

    def z_dev(d):
        return (me_r, 2 * lax.rem(z + d, chips) + k)

    barrier = pltpu.get_barrier_semaphore()
    peers = [row_dev(d) for d in range(1, rows)] + [z_dev(d) for d in range(1, chips)] + [sib]
    for dev in peers:
        pl.semaphore_signal(barrier, inc=1, device_id=dev, device_id_type=MESH)

    def g_copy(level):
        return pltpu.make_async_copy(g_hbm.at[level], g.at[level % kept], g_sem.at[level % kept])

    if kept == steps:
        for level in range(steps):
            g_copy(level).start()

    def g_ready(level, forward):
        if kept == steps:
            if forward:
                g_copy(level).wait()
        elif forward or level < steps - 1:
            g_copy(level).start()
            g_copy(level).wait()

    started = []

    def send(src, dst, s_sem, r_sem, dev):
        copy = pltpu.make_async_remote_copy(
            src_ref=src, dst_ref=dst, send_sem=s_sem, recv_sem=r_sem,
            device_id=dev, device_id_type=MESH,
        )
        copy.start()
        started.append(copy)

    def arrived(dst, s_sem, r_sem):
        pltpu.make_async_remote_copy(
            src_ref=dst, dst_ref=dst, send_sem=s_sem, recv_sem=r_sem,
            device_id=sib, device_id_type=MESH,
        ).wait_recv()

    def lanes(h):
        return slice(h * n, (h + 1) * n)

    def wide(x):
        return jnp.concatenate(split(x), axis=1)

    def left(a, w):
        p = dot(a, w)
        return (p[:S, :n] + p[:S, n:]) + (p[S:, :n] + p[S:, n:])

    def right(v, high, low):
        vh, vl = split(v)
        p = dot(jnp.concatenate([vh, vl], axis=0), high)
        return p[:n] + p[n:] + dot(vh, low)

    def forward_solve(level, h, v):
        d2 = jnp.concatenate(split(dinv[level, 0, 0]), axis=0)
        y = left(d2, wide(v))
        if level < steps:
            fg[level, h, me_r] = y
            if level == 0 and h == 0:
                pl.semaphore_wait(barrier, len(peers))
            for d in range(1, rows):
                ref = fg.at[level, h, me_r]
                send(ref, ref, row_s.at[level, h, d], row_r.at[level, h, d], row_dev(d))
        f_out[level, 0, 0, :, lanes(h)] = y
        yt[level, h] = y.T

    for h in range(halves):
        forward_solve(0, h, rhs[0, 0, 0, :, lanes(h)])

    for l in range(steps):
        g_ready(l, True)
        for h in range(halves):
            for d in range(1, rows):
                frm = lax.rem(me_r + rows - d, rows)
                arrived(fg.at[l, h, frm], row_s.at[l, h, d], row_r.at[l, h, d])
            w = wide(fg[l, h].reshape(rows * S, n))

            def term(t):
                return left(g[l % kept, t].reshape(2 * S, rows * S), w)

            def for_sib(c, _):
                psib[l, h, c] = term(2 * c + 1 - k)
                return 0

            def for_own(c, _):
                pown[l, h, c] = term(2 * c + k)
                return 0

            lax.fori_loop(0, chips, for_sib, 0, unroll=unroll)
            send(psib.at[l, h], rsib.at[l, h], sib_s.at[l, h], sib_r.at[l, h], sib)
            lax.fori_loop(0, chips, for_own, 0, unroll=unroll)
            arrived(rsib.at[l, h], sib_s.at[l, h], sib_r.at[l, h])
            for d in range(1, chips):
                c = lax.rem(z + d, chips)
                pown[l, h, c] += rsib[l, h, c]
                send(pown.at[l, h, c], rz.at[l, h, d], z_s.at[l, h, d], z_r.at[l, h, d], z_dev(d))
        for h in range(halves):
            u = pown[l, h, z] + rsib[l, h, z]
            for d in range(1, chips):
                arrived(rz.at[l, h, d], z_s.at[l, h, d], z_r.at[l, h, d])
                u += rz[l, h, d]
            forward_solve(l + 1, h, rhs[l + 1, 0, 0, :, lanes(h)] - u)

    def backward_solve(level, h, v):
        x = right(v, *split(dinv[level, 0, 0]))
        if level > 0:
            l = level - 1
            zg[l, h, me_c] = x
            ref = zg.at[l, h, me_c]
            for d in range(1, chips):
                send(ref, ref, bz_s.at[l, h, d], bz_r.at[l, h, d], z_dev(d))
            send(ref, ref, bsib_s.at[l, h, 0], bsib_r.at[l, h, 0], sib)
        s_out[level, 0, 0, :, lanes(h)] = x.T

    for h in range(halves):
        backward_solve(steps, h, yt[steps, h])

    for l in range(steps - 1, -1, -1):
        g_ready(l, False)
        for h in range(halves):
            def add(c, first):
                v = jnp.concatenate([zg[l, h, 2 * c], zg[l, h, 2 * c + 1]], axis=1)
                high = jnp.concatenate([g[l % kept, 2 * c, 0], g[l % kept, 2 * c + 1, 0]], axis=0)
                low = jnp.concatenate([g[l % kept, 2 * c, 1], g[l % kept, 2 * c + 1, 1]], axis=0)
                p = right(v, high, low)
                for s in range(rows):
                    part = p[:, s * S : (s + 1) * S]
                    q[l, h, s] = part if first else q[l, h, s] + part

            arrived(zg.at[l, h, 2 * z + 1 - k], bsib_s.at[l, h, 0], bsib_r.at[l, h, 0])
            add(z, True)
            for d in range(1, chips):
                c = lax.rem(z + chips - d, chips)
                ref = zg.at[l, h, 2 * c + k]
                arrived(ref, bz_s.at[l, h, d], bz_r.at[l, h, d])
                send(ref, ref, bsib_s.at[l, h, d], bsib_r.at[l, h, d], sib)
            for d in range(1, chips):
                c = lax.rem(z + chips - d, chips)
                arrived(zg.at[l, h, 2 * c + 1 - k], bsib_s.at[l, h, d], bsib_r.at[l, h, d])
                add(c, False)
            for d in range(1, rows):
                to = lax.rem(me_r + d, rows)
                send(q.at[l, h, to], rq.at[l, h, d], brow_s.at[l, h, d], brow_r.at[l, h, d], row_dev(d))
        for h in range(halves):
            u = q[l, h, me_r]
            for d in range(1, rows):
                arrived(rq.at[l, h, d], brow_s.at[l, h, d], brow_r.at[l, h, d])
                u += rq[l, h, d]
            backward_solve(l, h, yt[l, h] - u)

    for copy in started:
        copy.wait_send()


def solve(rhs, dinv, g, rows, cols):
    levels, _, _, S, total = rhs.shape
    halves = 2
    n = total // halves
    steps, chips = levels - 1, cols // 2
    kept = steps if rows * cols <= 64 else 1

    def vmem(*shape):
        return pltpu.VMEM(shape, F32)

    def sems(*shape):
        return [pltpu.SemaphoreType.DMA(shape)] * 2

    whole = pl.BlockSpec(memory_space=pltpu.VMEM)
    out = jax.ShapeDtypeStruct(rhs.shape, F32)
    return pl.pallas_call(
        functools.partial(solve_kernel, rows, cols, halves),
        out_shape=(out, out),
        in_specs=[whole, whole, pl.BlockSpec(memory_space=pl.ANY)],
        out_specs=(whole, whole),
        scratch_shapes=[
            pltpu.VMEM((kept,) + g.shape[1:], BF16),
            vmem(steps, halves, rows, S, n),
            vmem(steps, halves, chips, S, n),
            vmem(steps, halves, chips, S, n),
            vmem(steps, halves, chips, S, n),
            vmem(steps, halves, chips, S, n),
            vmem(steps, halves, cols, n, S),
            vmem(steps, halves, rows, n, S),
            vmem(steps, halves, rows, n, S),
            vmem(levels, halves, n, S),
            pltpu.SemaphoreType.DMA((kept,)),
            *sems(steps, halves, rows),
            *sems(steps, halves),
            *sems(steps, halves, chips),
            *sems(steps, halves, chips),
            *sems(steps, halves, chips),
            *sems(steps, halves, rows),
        ],
        compiler_params=pltpu.CompilerParams(
            collective_id=0, has_side_effects=True, vmem_limit_bytes=VMEM_BYTES
        ),
    )(rhs, dinv, g)


def solution(mesh):
    rows, cols = mesh.shape["row"], mesh.shape["col"]

    def per_device(rhs, diag_inverse, update_blocks, source_slot, target_slot, block_count):
        g = merge(
            update_blocks[:, 0, 0], source_slot[:, 0, 0], target_slot[:, 0, 0],
            block_count[:, 0, 0], rows, cols,
        )
        return solve(rhs, diag_inverse, g, rows, cols)

    in_specs = (
        P(None, "row", "col", None, None),
        P(None, "row", "col", None, None),
        P(None, "row", "col", None, None, None),
        P(None, "row", "col", None),
        P(None, "row", "col", None),
        P(None, "row", "col"),
    )
    out_specs = (P(None, "row", "col", None, None), P(None, "row", "col", None, None))
    return jax.shard_map(
        per_device, mesh=mesh, in_specs=in_specs, out_specs=out_specs, check_vma=False
    )
```

time: 545 us -> 124 us (0.23)
  waiting for transfers between devices: 332 us -> 0 us
  Pallas kernels: 0 us -> 118 us
  other arithmetic: 55.7 us -> 0 us
  local copies, waits for them, and re-layouts: 55.2 us -> 5.02 us
  matrix products: 48.8 us -> 0 us
  blocking collectives: 32 us -> 0 us
  between operations: 16 us -> 0.64 us
    reduce_scatter x3 -> x0, waiting for transfers between devices: 140 us -> none  [per_device(): lax.psum_scatter(block_terms(tiles_local[level_index - 1], sources_local[...]
    unnamed x12 -> x0, waiting for transfers between devices: 121 us -> none
    pallas_call x0 -> x2, Pallas kernels: none -> 118 us  [the longest x1 111 us: solve(): pl.pallas_call(functools.partial(solve_kernel, rows, cols, halves), out_s...]
    all_gather x3 -> x0, waiting for transfers between devices: 70.5 us -> none  [per_device(): gathered = lax.all_gather(backward[0][None], 'col', axis=0, tiled=True)]
    dot_general x26 -> x0, matrix products: 48.8 us -> none  [the longest x9 19.2 us: advance(): jnp.einsum('gst,gtn->gsn', tile_group, selected, precision=lax.Precision....]
    scatter-add x18 -> x0, other arithmetic: 41.4 us -> none  [advance(): return running.at[target_rows].add(products * active[:, None, None])]
    all_gather x3 -> x0, blocking collectives: 32 us -> none  [per_device(): lax.all_gather(forward[-1][None], 'row', axis=0, tiled=True)]
    gather x18 -> x0, local copies, waits for them, and re-layouts: 22.1 us -> none  [advance(): selected = operand[chosen_rows]]
  transfers between devices with their start and end apart: 9 -> 0, of which waited for: 9 -> 0; matrix products, arithmetic and copies ran while one was open for 1% -> 0% of each run, Pallas kernels for 0% -> 0%
where the time goes in v1:
time: 124 us
  Pallas kernels  118 us (95%)
  local copies, waits for them, and re-layouts  5.02 us (4%)
    pallas_call x1, Pallas kernels, solve(): pl.pallas_call(functools.partial(solve_kernel, rows, cols, halves), out_s...  111 us
    pallas_call x1, Pallas kernels, merge(): pl.pallas_call(functools.partial(merge_kernel, rows, per), grid=(steps, p...  7.14 us
    unnamed x3, local copies, waits for them, and re-layouts  5.02 us

profile of v1, /device:TPU:0, one launch (start us, length us, event | category | flops | bytes accessed | tf_op | source)
XLA Modules:
  0.0 123.8 jit_solution(13220318279894846324)
XLA Ops:
  0.6 1.3 %copy_bitcast_fusion = (s32[3,48]{1,0:T(4,128)}, s32[3,48]{1,0:T(4,128)}) fusion(s32[3,1,1,48]{3,2,1,0:T(1,128)} %param.10, s32[3,1,1,48]{3,2,1,0:T(1,128)} %param.9), kind=kLoop, calls=%fused_computation | loop fusion | bytes 2304
  1.9 7.1 %shard_map.77.g_hbm = bf16[3,8,2,128,512]{4,3,2,1,0:T(8,128)(2,1)} custom-call(s32[3,48]{1,0:T(4,128)} %get-tuple-element.3.src, s32[3,48]{1,0:T(4,128)} %get-tuple-element.2.tgt, s32[3]{0:T(128)} %bitcast.7, f32[3,48,128,128]{3,2,1,0:T(8,128)} %bitcast.6), custom_call_target="tpu_custom_call" | custom-call | tf_op jit(solution)/shard_map/pallas_call | solution.py:56
  9.0 111.0 %shard_map.78 = (f32[4,1,1,128,256]{4,3,2,1,0:T(8,128)}, f32[4,1,1,128,256]{4,3,2,1,0:T(8,128)}) custom-call(f32[4,1,1,128,256]{4,3,2,1,0:T(8,128)} %rhs.1, f32[4,1,1,128,128]{4,3,2,1,0:T(8,128)} %dinv.1, bf16[3,8,2,128,512]{4,3,2,1,0:T(8,128)(2,1)} %shard_map.77.g_hbm), custom_call_target="tpu_custom_call" | custom-call | tf_op jit(solution)/shard_map/pallas_call | solution.py:257
  120.1 1.9 %copy.14 = f32[4,1,1,128,256]{4,3,2,1,0:T(8,128)} copy(f32[4,1,1,128,256]{4,3,2,1,0:T(8,128)} %get-tuple-element.6) | data formatting | bytes 1048576
  121.9 1.9 %copy.15 = f32[4,1,1,128,256]{4,3,2,1,0:T(8,128)} copy(f32[4,1,1,128,256]{4,3,2,1,0:T(8,128)} %get-tuple-element.7) | data formatting | bytes 1048576

commit v2 on v1

--- a/solution.py
+++ b/solution.py
@@ -27,17 +27,17 @@
     acc[...] = jnp.zeros_like(acc)
 
     def add(b, _):
-        t = tgt[level, b] - part * cols
-        s = src[level, b]
+        t = tgt[level, 0, 0, b] - part * cols
+        s = src[level, 0, 0, b]
 
         @pl.when((t >= 0) & (t < cols))
         def _():
             i = t * rows + s
-            acc[i] += blocks[0, b]
+            acc[i] += blocks[b]
 
         return 0
 
-    lax.fori_loop(0, count[level], add, 0)
+    lax.fori_loop(0, count[level, 0, 0], add, 0)
 
     def write(t, _):
         for s in range(rows):
@@ -50,7 +50,7 @@
 
 
 def merge(blocks, src, tgt, count, rows, cols):
-    steps, slots, width, _ = blocks.shape
+    steps, _, _, slots, width, _ = blocks.shape
     parts = max(1, rows * cols // 64)
     per = cols // parts
     return pl.pallas_call(
@@ -58,7 +58,7 @@
         grid=(steps, parts),
         out_shape=jax.ShapeDtypeStruct((steps, cols, 2, width, rows * width), BF16),
         in_specs=[pl.BlockSpec(memory_space=pltpu.SMEM)] * 3
-        + [pl.BlockSpec((1, slots, width, width), lambda l, p: (l, 0, 0, 0))],
+        + [pl.BlockSpec((None, None, None, slots, width, width), lambda l, p: (l, 0, 0, 0, 0, 0))],
         out_specs=pl.BlockSpec((1, per, 2, width, rows * width), lambda l, p: (l, p, 0, 0, 0)),
         scratch_shapes=[pltpu.VMEM((per * rows, width, width), F32)],
         compiler_params=pltpu.CompilerParams(vmem_limit_bytes=VMEM_BYTES),
@@ -151,42 +151,38 @@
         f_out[level, 0, 0, :, lanes(h)] = y
         yt[level, h] = y.T
 
-    for h in range(halves):
-        forward_solve(0, h, rhs[0, 0, 0, :, lanes(h)])
-
-    for l in range(steps):
-        g_ready(l, True)
-        for h in range(halves):
-            for d in range(1, rows):
-                frm = lax.rem(me_r + rows - d, rows)
-                arrived(fg.at[l, h, frm], row_s.at[l, h, d], row_r.at[l, h, d])
-            w = wide(fg[l, h].reshape(rows * S, n))
-
-            def term(t):
-                return left(g[l % kept, t].reshape(2 * S, rows * S), w)
-
-            def for_sib(c, _):
-                psib[l, h, c] = term(2 * c + 1 - k)
-                return 0
-
-            def for_own(c, _):
-                pown[l, h, c] = term(2 * c + k)
-                return 0
-
-            lax.fori_loop(0, chips, for_sib, 0, unroll=unroll)
-            send(psib.at[l, h], rsib.at[l, h], sib_s.at[l, h], sib_r.at[l, h], sib)
-            lax.fori_loop(0, chips, for_own, 0, unroll=unroll)
-            arrived(rsib.at[l, h], sib_s.at[l, h], sib_r.at[l, h])
-            for d in range(1, chips):
-                c = lax.rem(z + d, chips)
-                pown[l, h, c] += rsib[l, h, c]
-                send(pown.at[l, h, c], rz.at[l, h, d], z_s.at[l, h, d], z_r.at[l, h, d], z_dev(d))
-        for h in range(halves):
-            u = pown[l, h, z] + rsib[l, h, z]
-            for d in range(1, chips):
-                arrived(rz.at[l, h, d], z_s.at[l, h, d], z_r.at[l, h, d])
-                u += rz[l, h, d]
-            forward_solve(l + 1, h, rhs[l + 1, 0, 0, :, lanes(h)] - u)
+    def forward_products(l, h):
+        for d in range(1, rows):
+            frm = lax.rem(me_r + rows - d, rows)
+            arrived(fg.at[l, h, frm], row_s.at[l, h, d], row_r.at[l, h, d])
+        w = wide(fg[l, h].reshape(rows * S, n))
+
+        def term(t):
+            return left(g[l % kept, t].reshape(2 * S, rows * S), w)
+
+        def for_sib(c, _):
+            psib[l, h, c] = term(2 * c + 1 - k)
+            return 0
+
+        def for_own(c, _):
+            pown[l, h, c] = term(2 * c + k)
+            return 0
+
+        lax.fori_loop(0, chips, for_sib, 0, unroll=unroll)
+        send(psib.at[l, h], rsib.at[l, h], sib_s.at[l, h], sib_r.at[l, h], sib)
+        lax.fori_loop(0, chips, for_own, 0, unroll=unroll)
+        arrived(rsib.at[l, h], sib_s.at[l, h], sib_r.at[l, h])
+        for d in range(1, chips):
+            c = lax.rem(z + d, chips)
+            pown[l, h, c] += rsib[l, h, c]
+            send(pown.at[l, h, c], rz.at[l, h, d], z_s.at[l, h, d], z_r.at[l, h, d], z_dev(d))
+
+    def forward_next(l, h):
+        u = pown[l, h, z] + rsib[l, h, z]
+        for d in range(1, chips):
+            arrived(rz.at[l, h, d], z_s.at[l, h, d], z_r.at[l, h, d])
+            u += rz[l, h, d]
+        forward_solve(l + 1, h, rhs[l + 1, 0, 0, :, lanes(h)] - u)
 
     def backward_solve(level, h, v):
         x = right(v, *split(dinv[level, 0, 0]))
@@ -199,41 +195,58 @@
             send(ref, ref, bsib_s.at[l, h, 0], bsib_r.at[l, h, 0], sib)
         s_out[level, 0, 0, :, lanes(h)] = x.T
 
+    def backward_products(l, h):
+        def add(c, first):
+            v = jnp.concatenate([zg[l, h, 2 * c], zg[l, h, 2 * c + 1]], axis=1)
+            high = jnp.concatenate([g[l % kept, 2 * c, 0], g[l % kept, 2 * c + 1, 0]], axis=0)
+            low = jnp.concatenate([g[l % kept, 2 * c, 1], g[l % kept, 2 * c + 1, 1]], axis=0)
+            p = right(v, high, low)
+            for s in range(rows):
+                part = p[:, s * S : (s + 1) * S]
+                q[l, h, s] = part if first else q[l, h, s] + part
+
+        arrived(zg.at[l, h, 2 * z + 1 - k], bsib_s.at[l, h, 0], bsib_r.at[l, h, 0])
+        add(z, True)
+        for d in range(1, chips):
+            c = lax.rem(z + chips - d, chips)
+            ref = zg.at[l, h, 2 * c + k]
+            arrived(ref, bz_s.at[l, h, d], bz_r.at[l, h, d])
+            send(ref, ref, bsib_s.at[l, h, d], bsib_r.at[l, h, d], sib)
+        for d in range(1, chips):
+            c = lax.rem(z + chips - d, chips)
+            arrived(zg.at[l, h, 2 * c + 1 - k], bsib_s.at[l, h, d], bsib_r.at[l, h, d])
+            add(c, False)
+        for d in range(1, rows):
+            to = lax.rem(me_r + d, rows)
+            send(q.at[l, h, to], rq.at[l, h, d], brow_s.at[l, h, d], brow_r.at[l, h, d], row_dev(d))
+
+    def backward_next(l, h):
+        u = q[l, h, me_r]
+        for d in range(1, rows):
+            arrived(rq.at[l, h, d], brow_s.at[l, h, d], brow_r.at[l, h, d])
+            u += rq[l, h, d]
+        backward_solve(l, h, yt[l, h] - u)
+
     for h in range(halves):
-        backward_solve(steps, h, yt[steps, h])
-
+        forward_solve(0, h, rhs[0, 0, 0, :, lanes(h)])
+    g_ready(0, True)
+    for h in range(halves):
+        forward_products(0, h)
+    for l in range(steps):
+        if l + 1 < steps:
+            g_ready(l + 1, True)
+        for h in range(halves):
+            forward_next(l, h)
+            if l + 1 < steps:
+                forward_products(l + 1, h)
+            else:
+                backward_solve(steps, h, yt[steps, h])
     for l in range(steps - 1, -1, -1):
         g_ready(l, False)
         for h in range(halves):
-            def add(c, first):
-                v = jnp.concatenate([zg[l, h, 2 * c], zg[l, h, 2 * c + 1]], axis=1)
-                high = jnp.concatenate([g[l % kept, 2 * c, 0], g[l % kept, 2 * c + 1, 0]], axis=0)
-                low = jnp.concatenate([g[l % kept, 2 * c, 1], g[l % kept, 2 * c + 1, 1]], axis=0)
-                p = right(v, high, low)
-                for s in range(rows):
-                    part = p[:, s * S : (s + 1) * S]
-                    q[l, h, s] = part if first else q[l, h, s] + part
-
-            arrived(zg.at[l, h, 2 * z + 1 - k], bsib_s.at[l, h, 0], bsib_r.at[l, h, 0])
-            add(z, True)
-            for d in range(1, chips):
-                c = lax.rem(z + chips - d, chips)
-                ref = zg.at[l, h, 2 * c + k]
-                arrived(ref, bz_s.at[l, h, d], bz_r.at[l, h, d])
-                send(ref, ref, bsib_s.at[l, h, d], bsib_r.at[l, h, d], sib)
-            for d in range(1, chips):
-                c = lax.rem(z + chips - d, chips)
-                arrived(zg.at[l, h, 2 * c + 1 - k], bsib_s.at[l, h, d], bsib_r.at[l, h, d])
-                add(c, False)
-            for d in range(1, rows):
-                to = lax.rem(me_r + d, rows)
-                send(q.at[l, h, to], rq.at[l, h, d], brow_s.at[l, h, d], brow_r.at[l, h, d], row_dev(d))
+            backward_products(l, h)
         for h in range(halves):
-            u = q[l, h, me_r]
-            for d in range(1, rows):
-                arrived(rq.at[l, h, d], brow_s.at[l, h, d], brow_r.at[l, h, d])
-                u += rq[l, h, d]
-            backward_solve(l, h, yt[l, h] - u)
+            backward_next(l, h)
 
     for copy in started:
         copy.wait_send()
@@ -284,15 +297,28 @@
     )(rhs, dinv, g)
 
 
+def place_kernel(f_in, s_in, f_out, s_out):
+    f_out[...] = f_in[...]
+    s_out[...] = s_in[...]
+
+
+def place(f, s):
+    block = pl.BlockSpec((2,) + f.shape[1:], lambda l: (l, 0, 0, 0, 0))
+    out = jax.ShapeDtypeStruct(f.shape, F32)
+    return pl.pallas_call(
+        place_kernel, grid=(f.shape[0] // 2,), out_shape=(out, out),
+        in_specs=[block, block], out_specs=(block, block),
+    )(f, s)
+
+
 def solution(mesh):
     rows, cols = mesh.shape["row"], mesh.shape["col"]
 
     def per_device(rhs, diag_inverse, update_blocks, source_slot, target_slot, block_count):
         g = merge(
-            update_blocks[:, 0, 0], source_slot[:, 0, 0], target_slot[:, 0, 0],
-            block_count[:, 0, 0], rows, cols,
+            update_blocks, source_slot, target_slot, block_count, rows, cols,
         )
-        return solve(rhs, diag_inverse, g, rows, cols)
+        return place(*solve(rhs, diag_inverse, g, rows, cols))
 
     in_specs = (
         P(None, "row", "col", None, None),

time: 124 us -> 121 us (0.976)
  local copies, waits for them, and re-layouts: 5.02 us -> 1.3 us
    unnamed x3 -> x1, local copies, waits for them, and re-layouts: 5.02 us -> 1.3 us
    pallas_call x0 -> x1, Pallas kernels: none -> 2.04 us  [place(): pl.pallas_call(place_kernel, grid=(f.shape[0] // 2,), out_shape=(out, out...]
    pallas_call x1, Pallas kernels: 111 us -> 109 us  [solve(): pl.pallas_call(functools.partial(solve_kernel, rows, cols, halves), out_s...]
where the time goes in v2:
time: 121 us
  Pallas kernels  119 us (98%)
  local copies, waits for them, and re-layouts  1.3 us (1%)
    pallas_call x1, Pallas kernels, solve(): pl.pallas_call(functools.partial(solve_kernel, rows, cols, halves), out_s...  109 us
    pallas_call x1, Pallas kernels, merge(): pl.pallas_call(functools.partial(merge_kernel, rows, per), grid=(steps, p...  7.76 us

profile of v2, /device:TPU:0, one launch (start us, length us, event | category | flops | bytes accessed | tf_op | source)
XLA Modules:
  0.0 120.9 jit_solution(16525662875225892217)
XLA Ops:
  0.6 1.3 %copy.8.count = s32[3,1,1]{2,1,0:T(1,128)} copy(s32[3,1,1]{0,2,1:T(1,128)} %param.11) | data formatting | bytes 24 | tf_op args[5]
  1.9 7.8 %shard_map.77.g_hbm = bf16[3,8,2,128,512]{4,3,2,1,0:T(8,128)(2,1)} custom-call(s32[3,1,1,48]{3,2,1,0:T(1,128)} %src.1, s32[3,1,1,48]{3,2,1,0:T(1,128)} %tgt.1, s32[3,1,1]{2,1,0:T(1,128)} %copy.8.count, f32[3,1,1,48,128,128]{5,4,3,2,1,0:T(8,128)} %blocks.1), custom_call_target="tpu_custom_call" | custom-call | tf_op jit(solution)/shard_map/pallas_call | solution.py:56
  9.7 109.1 %shard_map.78 = (f32[4,1,1,128,256]{4,3,2,1,0:T(8,128)}, f32[4,1,1,128,256]{4,3,2,1,0:T(8,128)}) custom-call(f32[4,1,1,128,256]{4,3,2,1,0:T(8,128)} %rhs.1, f32[4,1,1,128,128]{4,3,2,1,0:T(8,128)} %dinv.1, bf16[3,8,2,128,512]{4,3,2,1,0:T(8,128)(2,1)} %shard_map.77.g_hbm), custom_call_target="tpu_custom_call" | custom-call | tf_op jit(solution)/shard_map/pallas_call | solution.py:270
  118.8 2.0 %shard_map.79 = (f32[4,1,1,128,256]{4,3,2,1,0:T(8,128)}, f32[4,1,1,128,256]{4,3,2,1,0:T(8,128)}) custom-call(f32[4,1,1,128,256]{4,3,2,1,0:T(8,128)} %get-tuple-element.4.f_in, f32[4,1,1,128,256]{4,3,2,1,0:T(8,128)} %get-tuple-element.5.s_in), custom_call_target="tpu_custom_call" | custom-call | tf_op jit(solution)/shard_map/pallas_call | solution.py:308
